TPU v7x, 512 devices: a whole 4x8x8 slice. The times are simulated.
512 devices in a mesh: blk: 64 (over z_lo, y, core), grp: 8 (over z_hi, x).
Axes of the slice: x: 4, y: 8, z: 8 (z_hi: 2, z_lo: 4; z = z_hi * 4 + z_lo), core: 2. Of those that a mesh axis runs over, the one named last changes fastest.
Arguments:
- feats: bfloat16 [256, 131072], P('grp', 'blk'), may hold values from -6 to 6
- weight: bfloat16 [256, 256], replicated, may hold values from -0.375 to 0.375
- nbr: int32 [16, 131072], P('grp', 'blk'), may hold values from 0 to 131071, as said below
- mult: bfloat16 [16, 131072], P('grp', 'blk'), may hold values from 0.099609375 to 3
- cotan: bfloat16 [256, 131072], P('grp', 'blk'), may hold values from -6 to 6
Outputs:
- hidden: bfloat16 [256, 131072], P('grp', 'blk')
- grad_feats: float32 [256, 131072], P('grp', 'blk')
- grad_weight: float32 [256, 256], P('grp')
Inputs may be any that keep to these rules, and one draw needn't show every extreme that they name: `nbr`: the neighbours of a node in block b of 2048 nodes lie in blocks b, b - 1, ..., b - 3, counted cyclically over the 64 blocks. A program may pack these indices, or parts of them, several to a word for any transfer; this is an exception to the 16-bit rule below.
All inputs are finite; a program needn't handle non-finite values.
Results may differ from a plain program's by a relative error of at most 0.02.
Values may be sent and summed in bfloat16 or wider, within the bound.
A program may use at most 128 MiB of HBM per device.

v0:
```python
import jax
import jax.numpy as jnp
from jax import lax
from jax.sharding import PartitionSpec as P

BAND = 4


def shifted(value, axis, by):
    devices = lax.axis_size(axis)
    return lax.ppermute(value, axis, [(i, (i + by) % devices) for i in range(devices)])


def body(feats, weight, nbr, mult, cotan):
    feat_cols, rows_here = feats.shape
    blocks = lax.axis_size("blk")
    block_id = lax.axis_index("blk")
    group_id = lax.axis_index("grp")
    neighbours = lax.all_gather(nbr, "grp", axis=0, tiled=True)
    weights_all = lax.all_gather(mult, "grp", axis=0, tiled=True)
    edge_weight = weights_all.astype(jnp.float32)
    root_inv = lax.rsqrt(1.0 + jnp.sum(edge_weight, axis=0))
    scaled = (feats.astype(jnp.float32) * root_inv).astype(jnp.bfloat16)
    local_index = neighbours % rows_here
    offset = (block_id - neighbours // rows_here + blocks) % blocks
    node_ids = jnp.arange(rows_here, dtype=jnp.int32)

    def adjacency(step):
        masked = jnp.where(offset == step, edge_weight, 0.0)
        hits = local_index[:, None, :] == node_ids[None, :, None]
        return jnp.sum(jnp.where(hits, masked[:, None, :], 0.0), axis=0).astype(jnp.bfloat16)

    tiles = [adjacency(step) for step in range(BAND)]
    summed = scaled.astype(jnp.float32)
    visiting = scaled
    for step in range(BAND):
        if step > 0:
            visiting = shifted(visiting, "blk", 1)
        summed = summed + jnp.dot(visiting, tiles[step], preferred_element_type=jnp.float32)
    aggregated = (root_inv * summed).astype(jnp.bfloat16)
    w_rows = lax.dynamic_slice_in_dim(weight, group_id * feat_cols, feat_cols, 0)
    z_value = lax.psum_scatter(
        lax.dot_general(
            w_rows, aggregated, (((0,), (0,)), ((), ())), preferred_element_type=jnp.float32
        ).astype(jnp.bfloat16),
        "grp",
        scatter_dimension=0,
        tiled=True,
    ).astype(jnp.float32)
    hidden = jax.nn.silu(z_value).astype(jnp.bfloat16)
    logistic = jax.nn.sigmoid(z_value)
    grad_z = (cotan.astype(jnp.float32) * logistic * (1.0 + z_value * (1.0 - logistic))).astype(
        jnp.bfloat16
    )
    grad_all = lax.all_gather(grad_z, "grp", axis=0, tiled=True)
    weight_part = lax.dot_general(
        aggregated, grad_all, (((1,), (1,)), ((), ())), preferred_element_type=jnp.float32
    )
    grad_agg = jnp.dot(w_rows, grad_all, preferred_element_type=jnp.float32)
    scaled_low = (root_inv * grad_agg).astype(jnp.bfloat16)
    scaled_grad = scaled_low.astype(jnp.float32)
    grad_weight = lax.psum(weight_part, "blk") * (rows_here * blocks) ** (-0.5)

    def spread(step):
        return lax.dot_general(
            scaled_low, tiles[step], (((1,), (1,)), ((), ())), preferred_element_type=jnp.float32
        )

    carried = spread(BAND - 1)
    for step in range(BAND - 2, -1, -1):
        carried = shifted(carried.astype(jnp.bfloat16), "blk", -1).astype(carried.dtype)
        carried = carried + spread(step)
    grad_feats = root_inv * (scaled_grad + carried)
    return (hidden, grad_feats, grad_weight)


def solution(mesh):
    return jax.shard_map(
        body,
        mesh=mesh,
        in_specs=(P("grp", "blk"), P(), P("grp", "blk"), P("grp", "blk"), P("grp", "blk")),
        out_specs=(P("grp", "blk"), P("grp", "blk"), P("grp", None)),
        check_vma=False,
    )
```

profile of v0, /device:TPU:1, one launch (start us, length us, event | category | flops | bytes accessed | tf_op | source)
XLA Modules:
  0.0 771.5 jit_solution(8464668579550227921)
XLA Ops:
  7.2 42.4 %all-gather = bf16[8,2,2048]{2,1,0:T(2,128)(2,1)S(1)} all-gather(bf16[1,2,2048]{2,1,0:T(2,128)(2,1)} %bitcast.29), channel_id=1, replica_groups=mesh['blk'=64,'grp'=8] {'grp'}, dimensions={0}, use_global_device_ids=true | all-gather | bytes 73728 | tf_op jit(solution)/shard_map/all_gather | solution.py:20
  50.7 10.1 %collective-permute-start = (bf16[32,2048]{1,0:T(8,128)(2,1)S(1)}, bf16[32,2048]{1,0:T(8,128)(2,1)S(1)}, u32[]{:S(2)}, u32[]{:S(2)}) collective-permute-start(bf16[32,2048]{1,0:T(8,128)(2,1)S(1)} %multiply_convert_fusion), channel_id=1, source_target_pairs={{0,8},{8,16},{16,24},{24,32},{32,40},{40,48},{48,56},{56,64},{64,7... | collective-permute-start | bytes 393224 | tf_op jit(solution)/shard_map/ppermute | solution.py:11
  60.9 37.6 %all-gather.1 = s32[8,2,2048]{2,1,0:T(2,128)S(1)} all-gather(s32[1,2,2048]{2,1,0:T(2,128)} %bitcast.28), channel_id=1, replica_groups=mesh['blk'=64,'grp'=8] {'grp'}, dimensions={0}, use_global_device_ids=true | all-gather | bytes 147456 | tf_op jit(solution)/shard_map/all_gather | solution.py:19
  98.8 48.6 %select_reduce_fusion.3 = bf16[2048,2048]{1,0:T(8,128)(2,1)} fusion(f32[16,2048]{1,0:T(8,128)S(1)} %get-tuple-element.8, s32[16,2048]{1,0:T(8,128)S(1)} %add_select_fusion.2), kind=kLoop, calls=%fused_computation.3 | loop fusion | flops 197132288 | bytes 8650752 | tf_op jit(solution)/shard_map/reduce_sum | solution.py:31
  147.5 128.2 %select_reduce_fusion = (bf16[2048,2048]{1,0:T(8,128)(2,1)}, bf16[2048,2048]{1,0:T(8,128)(2,1)}, bf16[2048,2048]{1,0:T(8,128)(2,1)}) fusion(f32[16,2048]{1,0:T(8,128)S(1)} %get-tuple-element.9, s32[16,2048]{1,0:T(8,128)S(1)} %add_select_fusion.2, f32[16,2048]{1,0:T(8,128)S(1)} %get-tuple-element.7, f32[16,2048]{1,0:T(8,128)S(1)} %get-tuple-element.6), kind=kLoop, calls=%fused_computation | loop fusion | flops 457179136 | bytes 25690112 | tf_op jit(solution)/shard_map/reduce_sum | solution.py:31
  275.7 4.9 fusion.16
  280.6 8.5 %collective-permute-start.1 = (bf16[32,2048]{1,0:T(8,128)(2,1)S(1)}, bf16[32,2048]{1,0:T(8,128)(2,1)S(1)}, u32[]{:S(2)}, u32[]{:S(2)}) collective-permute-start(bf16[32,2048]{1,0:T(8,128)(2,1)S(1)} %collective-permute-done), channel_id=1, source_target_pairs={{0,8},{8,16},{16,24},{24,32},{32,40},{40,48},{48,56},{56,64},{64,7... | collective-permute-start | bytes 393224 | tf_op jit(solution)/shard_map/ppermute | solution.py:11
  289.1 4.9 fusion.19
  294.1 2.2 collective-permute-start.2
  296.3 5.1 fusion.22
  301.4 1.6 fusion.31
  303.0 1.4 convolution_convert_fusion
  304.5 91.0 %reduce-scatter.2.cloned.1.call-done = bf16[32,2048]{1,0:T(8,128)(2,1)} async-done(((bf16[256,2048]{1,0:T(8,128)(2,1)}), bf16[32,2048]{1,0:T(8,128)(2,1)}) %reduce-scatter.2.cloned.1.call-update) | async-done | bytes 131088 | tf_op jit(solution)/shard_map/reduce_scatter | solution.py:42
  395.6 1.7 fusion.44
  397.3 65.8 %all-gather.4.cloned.1.call-done = bf16[256,2048]{1,0:T(8,128)(2,1)} async-done(((bf16[32,2048]{1,0:T(8,128)(2,1)}), bf16[256,2048]{1,0:T(8,128)(2,1)}) %all-gather.4.cloned.1.call-update) | async-done | bytes 1048592 | tf_op jit(solution)/shard_map/all_gather | solution.py:55
  463.1 1.7 fusion.34
  464.8 6.1 fusion.35
  471.0 6.1 fusion.56
  477.1 4.5 collective-permute-start.3
  481.6 2.6 fusion.55
  485.2 2.6 add_convert_fusion.1
  487.8 2.4 collective-permute-start.4
  490.6 264.1 %psum.7 = f32[32,256]{1,0:T(8,128)S(1)} all-reduce(f32[32,256]{1,0:T(8,128)S(1)} %fusion.54), channel_id=1, replica_groups=mesh['blk'=64,'grp'=8] {'blk'}, use_global_device_ids=true, to_apply=%region_6.7 | all-reduce | flops 8192 | bytes 65536 | tf_op jit(solution)/shard_map/psum | solution.py:62
  754.7 8.1 %collective-permute-start.5 = (bf16[32,2048]{1,0:T(8,128)(2,1)S(1)}, bf16[32,2048]{1,0:T(8,128)(2,1)S(1)}, u32[]{:S(2)}, u32[]{:S(2)}) collective-permute-start(bf16[32,2048]{1,0:T(8,128)(2,1)S(1)} %add_convert_fusion), channel_id=1, source_target_pairs={{0,504},{8,0},{16,8},{24,16},{32,24},{40,32},{48,40},{56,48},{64,5... | collective-permute-start | bytes 393224 | tf_op jit(solution)/shard_map/ppermute | solution.py:11
  (42 shorter events, 4.7 us)
Async XLA Ops:
  7.2 295.8 %copy-start = (bf16[256,256]{1,0:T(8,128)(2,1)S(1)}, bf16[256,256]{1,0:T(8,128)(2,1)}, u32[]{:S(2)}) copy-start(bf16[256,256]{1,0:T(8,128)(2,1)} %param.6) | copy-start | bytes 393220
  7.2 388.4 %reduce-scatter.2.cloned.1.call-start = ((), (), s32[]{:S(2)}) async-start(), calls=%async_computation.1 | async-start | bytes 1179648 | tf_op jit(solution)/shard_map/reduce_scatter | solution.py:42
  50.7 229.9 %collective-permute-start = (bf16[32,2048]{1,0:T(8,128)(2,1)S(1)}, bf16[32,2048]{1,0:T(8,128)(2,1)S(1)}, u32[]{:S(2)}, u32[]{:S(2)}) collective-permute-start(bf16[32,2048]{1,0:T(8,128)(2,1)S(1)} %multiply_convert_fusion), channel_id=1, source_target_pairs={{0,8},{8,16},{16,24},{24,32},{32,40},{40,48},{48,56},{56,64},{64,7... | collective-permute-start | bytes 393224 | tf_op jit(solution)/shard_map/ppermute | solution.py:11
  280.6 13.4 %collective-permute-start.1 = (bf16[32,2048]{1,0:T(8,128)(2,1)S(1)}, bf16[32,2048]{1,0:T(8,128)(2,1)S(1)}, u32[]{:S(2)}, u32[]{:S(2)}) collective-permute-start(bf16[32,2048]{1,0:T(8,128)(2,1)S(1)} %collective-permute-done), channel_id=1, source_target_pairs={{0,8},{8,16},{16,24},{24,32},{32,40},{40,48},{48,56},{56,64},{64,7... | collective-permute-start | bytes 393224 | tf_op jit(solution)/shard_map/ppermute | solution.py:11
  294.1 7.3 slice-start.4
  294.1 7.3 collective-permute-start.2
  296.3 5.1 slice-start.5
  301.4 94.1 %copy-start.2 = (bf16[32,2048]{1,0:T(8,128)(2,1)S(1)}, bf16[32,2048]{1,0:T(8,128)(2,1)}, u32[]{:S(2)}) copy-start(bf16[32,2048]{1,0:T(8,128)(2,1)} %param.9) | copy-start | bytes 393220
  304.5 158.7 %all-gather.4.cloned.1.call-start = ((), (), s32[]{:S(2)}) async-start(), calls=%async_computation.2 | async-start | bytes 1179648 | tf_op jit(solution)/shard_map/all_gather | solution.py:55
  463.1 18.4 %slice-start.2 = ((s8[8388608]{0:T(1024)(128)(4,1)}), s8[4194304]{0:T(1024)(128)(4,1)S(1)}, s32[]{:S(2)}) async-start(s8[8388608]{0:T(1024)(128)(4,1)} %bitcast.24), calls=%async_computation.5 | async-start | bytes 8388608
  464.8 16.8 %slice-start.3 = ((s8[8388608]{0:T(1024)(128)(4,1)}), s8[4194304]{0:T(1024)(128)(4,1)S(1)}, s32[]{:S(2)}) async-start(s8[8388608]{0:T(1024)(128)(4,1)} %bitcast.24), calls=%async_computation.6 | async-start | bytes 8388608
  470.9 14.3 %slice-start = ((s8[8388608]{0:T(1024)(128)(4,1)}), s8[4194304]{0:T(1024)(128)(4,1)S(1)}, s32[]{:S(2)}) async-start(s8[8388608]{0:T(1024)(128)(4,1)} %bitcast.22), calls=%async_computation.3 | async-start | bytes 8388608
  477.1 8.2 %slice-start.1 = ((s8[8388608]{0:T(1024)(128)(4,1)}), s8[4194304]{0:T(1024)(128)(4,1)S(1)}, s32[]{:S(2)}) async-start(s8[8388608]{0:T(1024)(128)(4,1)} %bitcast.22), calls=%async_computation.4 | async-start | bytes 8388608
  477.1 13.1 %copy-start.1 = (bf16[256,2048]{1,0:T(8,128)(2,1)S(1)}, bf16[256,2048]{1,0:T(8,128)(2,1)}, u32[]{:S(2)}) copy-start(bf16[256,2048]{1,0:T(8,128)(2,1)} %all-gather.4.cloned.1.call-done) | copy-start | bytes 3145732
  477.1 8.1 %collective-permute-start.3 = (bf16[32,2048]{1,0:T(8,128)(2,1)S(1)}, bf16[32,2048]{1,0:T(8,128)(2,1)S(1)}, u32[]{:S(2)}, u32[]{:S(2)}) collective-permute-start(bf16[32,2048]{1,0:T(8,128)(2,1)S(1)} %fusion.35), channel_id=1, source_target_pairs={{0,504},{8,0},{16,8},{24,16},{32,24},{40,32},{48,40},{56,48},{64,5... | collective-permute-start | bytes 393224 | tf_op jit(solution)/shard_map/ppermute | solution.py:11
  487.8 266.9 %collective-permute-start.4 = (bf16[32,2048]{1,0:T(8,128)(2,1)S(1)}, bf16[32,2048]{1,0:T(8,128)(2,1)S(1)}, u32[]{:S(2)}, u32[]{:S(2)}) collective-permute-start(bf16[32,2048]{1,0:T(8,128)(2,1)S(1)} %add_convert_fusion.1), channel_id=1, source_target_pairs={{0,504},{8,0},{16,8},{24,16},{32,24},{40,32},{48,40},{56,48},{64,5... | collective-permute-start | bytes 393224 | tf_op jit(solution)/shard_map/ppermute | solution.py:11
  754.7 9.1 %collective-permute-start.5 = (bf16[32,2048]{1,0:T(8,128)(2,1)S(1)}, bf16[32,2048]{1,0:T(8,128)(2,1)S(1)}, u32[]{:S(2)}, u32[]{:S(2)}) collective-permute-start(bf16[32,2048]{1,0:T(8,128)(2,1)S(1)} %add_convert_fusion), channel_id=1, source_target_pairs={{0,504},{8,0},{16,8},{24,16},{32,24},{40,32},{48,40},{56,48},{64,5... | collective-permute-start | bytes 393224 | tf_op jit(solution)/shard_map/ppermute | solution.py:11
Sparse Core Ops, SparseCore 0:
  304.6 90.9 reduce-scatter.1
  399.8 63.2 all-gather.3
where the time goes:
time: 772 us; the launch traced here: 771 us
  blocking collectives  344 us (45%)
  other arithmetic  181 us (23%)
  waiting for transfers between devices  158 us (20%)
  matrix products  37.4 us (5%)
  starting transfers between devices  35.9 us (5%)
  between operations  14.3 us (2%)
    psum x1, blocking collectives, body(): grad_weight = lax.psum(weight_part, 'blk') * (rows_here * blocks) ** (-0.5)  264 us
    reduce_sum x2, other arithmetic, adjacency(): jnp.sum(jnp.where(hits, masked[:, None, :], 0.0), axis=0)  177 us
    reduce_scatter x1, waiting for transfers between devices, body(): lax.psum_scatter(lax.dot_general(w_rows, aggregated, (((0,), (0,)), ((),...  91 us
    all_gather x1, waiting for transfers between devices, body(): grad_all = lax.all_gather(grad_z, 'grp', axis=0, tiled=True)  65.8 us
    all_gather x1, blocking collectives, body(): weights_all = lax.all_gather(mult, 'grp', axis=0, tiled=True)  42.4 us
    all_gather x1, blocking collectives, body(): neighbours = lax.all_gather(nbr, 'grp', axis=0, tiled=True)  37.6 us
    ppermute x6, starting transfers between devices, shifted(): lax.ppermute(value, axis, [(i, (i + by) % devices) for i in range(devices)])  35.8 us
    dot_general x4, matrix products, spread(): lax.dot_general(scaled_low, tiles[step], (((1,), (1,)), ((), ())), prefer...  17.4 us
  transfers between devices with their start and end apart: 8, of which 4 were waited for; matrix products, arithmetic and copies ran while one was open for 25% of the time, Pallas kernels for 0%

commit v1 on v0

v1 whole, which is shorter than its diff:
```python
import functools

import jax
import jax.numpy as jnp
from jax import lax
from jax.experimental import pallas as pl
from jax.experimental.pallas import tpu as pltpu
from jax.sharding import PartitionSpec as P

BAND = 4
CORES = 2
RINGS = 8
BF = jnp.bfloat16
F32 = jnp.float32
MESH = pl.DeviceIdType.MESH
NT = (((1,), (1,)), ((), ()))
WORDS, MULTS, COTS, AGGS, SGS, HIDS, GWS, RSUM, ZSUM, RALL = range(10)


def kernel(
    shape,
    feats,
    weight,
    words,
    mults,
    cotan,
    hidden,
    grad_feats,
    grad_weight,
    gw,
    gm,
    cot_all,
    halo,
    agg_own,
    agg_all,
    sg_own,
    sg,
    hid_own,
    adj,
    e_lo,
    e_hi,
    e_m,
    root,
    w_t,
    part,
    arrived,
    gw_own,
    gw_in,
    t_own,
    t_in,
    u_own,
    u_in,
    v_own,
    v_in,
    send_sem,
    recv_sem,
    hsend,
    hrecv,
):
    blocks, groups, rings = shape
    feat, rows = feats.shape
    width = feat * groups
    slice_n = rows // groups
    spans = blocks // rings
    edge_rows = words.shape[0]
    b = lax.axis_index("blk")
    g = lax.axis_index("grp")
    core = lax.rem(b, CORES)
    ring = lax.rem(b // CORES, rings)
    z_lo = b // (CORES * rings)
    span = z_lo * CORES + core

    def grp_dev(q):
        return (b, q)

    def ring_dev(q):
        return ((z_lo * rings + q) * CORES + core, g)

    def span_dev(q):
        return (((q // CORES) * rings + ring) * CORES + lax.rem(q, CORES), g)

    def rows_of(q):
        return pl.ds(pl.multiple_of(q * feat, feat), feat)

    def nodes_of(q):
        return pl.ds(pl.multiple_of(q * slice_n, slice_n), slice_n)

    def edges_of(q):
        return pl.ds(pl.multiple_of(q * edge_rows, 16), edge_rows)

    plans = {
        WORDS: (grp_dev, g, groups, lambda q: words, lambda q: gw.at[edges_of(q), :]),
        MULTS: (grp_dev, g, groups, lambda q: mults, lambda q: gm.at[:, edges_of(q), :]),
        COTS: (grp_dev, g, groups, lambda q: cotan.at[:, nodes_of(q)], lambda q: cot_all.at[rows_of(q), :]),
        AGGS: (grp_dev, g, groups, lambda q: agg_own.at[:, nodes_of(q)], lambda q: agg_all.at[rows_of(q), :]),
        SGS: (grp_dev, g, groups, lambda q: sg_own.at[rows_of(q), :], lambda q: sg.at[:, nodes_of(q)]),
        HIDS: (grp_dev, g, groups, lambda q: hid_own.at[rows_of(q), :], lambda q: hidden.at[:, nodes_of(q)]),
        GWS: (grp_dev, g, groups, lambda q: gw_own.at[rows_of(q), :], lambda q: gw_in.at[q]),
        RSUM: (ring_dev, ring, rings, lambda q: t_own.at[q], lambda q: t_in.at[q]),
        ZSUM: (span_dev, span, spans, lambda q: u_own, lambda q: u_in.at[q]),
        RALL: (ring_dev, ring, rings, lambda q: v_own, lambda q: v_in.at[q]),
    }

    def out_copy(phase, q):
        dev, me, _, src, dst = plans[phase]
        return pltpu.make_async_remote_copy(
            src_ref=src(q),
            dst_ref=dst(me),
            send_sem=send_sem.at[phase, q],
            recv_sem=recv_sem.at[phase, me],
            device_id=dev(q),
            device_id_type=MESH,
        )

    def in_copy(phase, q):
        dev, me, _, src, dst = plans[phase]
        return pltpu.make_async_remote_copy(
            src_ref=src(q),
            dst_ref=dst(q),
            send_sem=send_sem.at[phase, q],
            recv_sem=recv_sem.at[phase, q],
            device_id=dev(q),
            device_id_type=MESH,
        )

    def each(phase, act):
        me, count = plans[phase][1], plans[phase][2]

        @pl.loop(1, count)
        def _(i):
            act(lax.rem(me + i, count))

    def send_all(phase):
        each(phase, lambda q: out_copy(phase, q).start())

    def wait_all(phase):
        each(phase, lambda q: in_copy(phase, q).wait_recv())

    def sent_all(phase):
        each(phase, lambda q: out_copy(phase, q).wait_send())

    def halo_copy(off):
        return pltpu.make_async_remote_copy(
            src_ref=halo.at[:, pl.ds(0, rows)],
            dst_ref=halo.at[:, pl.ds(off * rows, rows)],
            send_sem=hsend.at[0, off - 1],
            recv_sem=hrecv.at[0, off - 1],
            device_id=(lax.rem(b + off, blocks), g),
            device_id_type=MESH,
        )

    def back_copy(off):
        return pltpu.make_async_remote_copy(
            src_ref=part.at[off - 1],
            dst_ref=arrived.at[off - 1],
            send_sem=hsend.at[1, off - 1],
            recv_sem=hrecv.at[1, off - 1],
            device_id=(lax.rem(b - off + blocks, blocks), g),
            device_id_type=MESH,
        )

    barrier = pltpu.get_barrier_semaphore()

    def greet(dev):
        pl.semaphore_signal(barrier, inc=1, device_id=dev, device_id_type=MESH)

    for phase in (WORDS, RSUM, ZSUM):
        each(phase, lambda q, dev=plans[phase][0]: greet(dev(q)))
    for off in range(1, BAND):
        greet((lax.rem(b + off, blocks), g))
        greet((lax.rem(b - off + blocks, blocks), g))
    pl.semaphore_wait(barrier, groups - 1 + rings - 1 + spans - 1 + 2 * (BAND - 1))

    send_all(WORDS)
    send_all(MULTS)
    send_all(COTS)
    gw[edges_of(g), :] = words[...]
    gm[:, edges_of(g), :] = mults[...]
    cot_all[rows_of(g), :] = cotan[:, nodes_of(g)]
    w_t[...] = weight[...].astype(F32).T.astype(BF)
    wait_all(WORDS)
    wait_all(MULTS)

    half = gw.shape[0]
    for h in range(2):
        code = (gw[...] >> (16 * h)) & 0xFFFF
        at = pl.ds(h * half, half)
        e_lo[:, at] = (code & 255).astype(F32).T
        e_hi[:, at] = (code >> 8).astype(F32).T
        e_m[:, at] = gm[h].astype(F32).T
    edges = 2 * half
    fold = (
        lax.rem(lax.broadcasted_iota(jnp.int32, (edges, 128), 0), 16)
        == lax.rem(lax.broadcasted_iota(jnp.int32, (edges, 128), 1), 16)
    )
    fold = jnp.where(fold, 1.0, 0.0).astype(BF)
    degree = jnp.dot(e_m[...].astype(BF), fold, preferred_element_type=F32)
    pick = (
        lax.broadcasted_iota(jnp.int32, (8, 128), 0)
        == lax.broadcasted_iota(jnp.int32, (8, 128), 1) // 16
    )
    for c in range(rows // 128):
        line = jnp.sum(jnp.where(pick, degree[c * 8 : c * 8 + 8, :], 0.0), axis=0, keepdims=True)
        root[:, c * 128 : c * 128 + 128] = lax.rsqrt(1.0 + line)
    halo[:, pl.ds(0, rows)] = (feats[...].astype(F32) * root[...]).astype(BF)
    for off in range(1, BAND):
        halo_copy(off).start()

    hi_count = BAND * rows // 256
    sub = lax.broadcasted_iota(jnp.int32, (16, edges), 0)
    own_lane = lax.rem(lax.broadcasted_iota(jnp.int32, (16, edges), 1), 16) == sub
    sub_f = sub.astype(F32)

    @pl.loop(0, rows // 16)
    def _(t):
        one = pl.ds(t, 1)
        low = (jnp.broadcast_to(e_lo[one, :], (16, edges)) - sub_f).astype(BF)
        high = jnp.broadcast_to(e_hi[one, :], (16, edges)).astype(BF)
        amount = jnp.where(own_lane, jnp.broadcast_to(e_m[one, :], (16, edges)), 0.0).astype(BF)
        zero = jnp.zeros((16, edges), BF)
        ones = jnp.ones((16, edges), BF)
        right = jnp.concatenate(
            [jnp.where(low == jnp.asarray(16.0 * c, BF), ones, zero) for c in range(16)], axis=0
        )
        left = jnp.concatenate(
            [jnp.where(high == jnp.asarray(float(c), BF), amount, zero) for c in range(hi_count)],
            axis=0,
        )
        made = lax.dot_general(left, right, NT, preferred_element_type=F32).astype(BF)
        adj[pl.ds(pl.multiple_of(t * 16, 16), 16), :] = jnp.concatenate(
            [made[c * 16 : c * 16 + 16, :] for c in range(hi_count)], axis=1
        )

    for off in range(1, BAND):
        halo_copy(off).wait_recv()

    step_n = 256

    def forward(q):
        @pl.loop(0, slice_n // step_n)
        def _(i):
            at = pl.ds(pl.multiple_of(q * slice_n + i * step_n, step_n), step_n)
            total = halo[:, at].astype(F32) + lax.dot_general(
                halo[...], adj[at, :], NT, preferred_element_type=F32
            )
            agg_own[:, at] = (root[:, at] * total).astype(BF)

    def forward_send(q):
        forward(q)
        out_copy(AGGS, q).start()

    each(AGGS, forward_send)
    forward(g)
    agg_all[rows_of(g), :] = agg_own[:, nodes_of(g)]
    wait_all(AGGS)
    wait_all(COTS)

    z = jnp.dot(w_t[...], agg_all[...], preferred_element_type=F32)
    s = 1.0 / (1.0 + jnp.exp(-z))
    grad_z = (cot_all[...].astype(F32) * s * (1.0 + z * (1.0 - s))).astype(BF)
    grad_agg = jnp.dot(weight[...], grad_z, preferred_element_type=F32)
    sg_own[...] = (root[:, nodes_of(g)] * grad_agg).astype(BF)
    send_all(SGS)
    gw_own[...] = lax.dot_general(agg_all[...], grad_z, NT, preferred_element_type=F32)
    send_all(GWS)
    hid_own[...] = (z * s).astype(BF)
    send_all(HIDS)
    sg[:, nodes_of(g)] = sg_own[rows_of(g), :]
    gw_in[g] = gw_own[rows_of(g), :]
    hidden[:, nodes_of(g)] = hid_own[rows_of(g), :]
    wait_all(SGS)

    chunk = feat // (rings // 2)
    for off in range(BAND - 1, -1, -1):

        @pl.loop(0, rows // 256)
        def _(i, off=off):
            at = pl.ds(pl.multiple_of(i * 256, 256), 256)
            src = pl.ds(pl.multiple_of(off * rows + i * 256, 256), 256)
            value = jnp.dot(sg[...], adj[:, src], preferred_element_type=F32)
            if off > 0:
                part[off - 1, :, at] = value.astype(BF)
            else:
                grad_feats[:, at] = value + sg[:, at].astype(F32)

        if off > 0:
            back_copy(off).start()
        if off == 3:
            wait_all(GWS)
            total = gw_in[0]
            for q in range(1, groups):
                total = total + gw_in[q]
            for q in range(rings):
                t_own[q] = total[
                    (q // 2) * chunk : (q // 2 + 1) * chunk, (q % 2) * 128 : (q % 2) * 128 + 128
                ]
            send_all(RSUM)
            t_in[ring] = t_own[ring]
        elif off == 2:
            wait_all(RSUM)
            total = t_in[0]
            for q in range(1, rings):
                total = total + t_in[q]
            u_own[...] = total
            send_all(ZSUM)
            u_in[span] = u_own[...]
        elif off == 1:
            wait_all(ZSUM)
            total = u_in[0]
            for q in range(1, spans):
                total = total + u_in[q]
            v_own[...] = total * (rows * blocks) ** (-0.5)
            send_all(RALL)
            v_in[ring] = v_own[...]

    wait_all(RALL)
    for q in range(rings):
        grad_weight[
            (q // 2) * chunk : (q // 2 + 1) * chunk, (q % 2) * 128 : (q % 2) * 128 + 128
        ] = v_in[q]
    for off in range(1, BAND):
        back_copy(off).wait_recv()
    carried = arrived[0].astype(F32)
    for off in range(2, BAND):
        carried = carried + arrived[off - 1].astype(F32)
    grad_feats[...] = root[...] * (grad_feats[...] + carried)
    wait_all(HIDS)
    for phase in plans:
        sent_all(phase)
    for off in range(1, BAND):
        halo_copy(off).wait_send()
        back_copy(off).wait_send()


def body(rings, feats, weight, nbr, mult, cotan):
    feat, rows = feats.shape
    slots = nbr.shape[0]
    blocks = lax.axis_size("blk")
    groups = lax.axis_size("grp")
    width = feat * groups
    slice_n = rows // groups
    b = lax.axis_index("blk")
    code = ((b - nbr // rows + blocks) % blocks) * rows + nbr % rows
    code = code.reshape(slots // 2, 2, rows // 16, 16)
    words = (code[:, 0] + code[:, 1] * 65536).transpose(0, 2, 1).reshape(slots * 8, rows // 16)
    mults = mult.reshape(slots // 2, 2, rows // 16, 16).transpose(1, 0, 3, 2)
    mults = mults.reshape(2, slots * 8, rows // 16)
    chunk = feat // (rings // 2)
    spans = blocks // rings
    vmem = pltpu.VMEM
    edges = 256
    most = max(groups, rings, spans)
    return tuple(
        pl.pallas_call(
            functools.partial(kernel, (blocks, groups, rings)),
            out_shape=(
                jax.ShapeDtypeStruct((feat, rows), BF),
                jax.ShapeDtypeStruct((feat, rows), F32),
                jax.ShapeDtypeStruct((feat, width), F32),
            ),
            in_specs=[pl.BlockSpec(memory_space=vmem)] * 5,
            out_specs=(pl.BlockSpec(memory_space=vmem),) * 3,
            scratch_shapes=[
                vmem((edges // 2, 128), jnp.int32),
                vmem((2, edges // 2, 128), BF),
                vmem((width, slice_n), BF),
                vmem((feat, BAND * rows), BF),
                vmem((feat, rows), BF),
                vmem((width, slice_n), BF),
                vmem((width, slice_n), BF),
                vmem((feat, rows), BF),
                vmem((width, slice_n), BF),
                vmem((rows, BAND * rows), BF),
                vmem((128, edges), F32),
                vmem((128, edges), F32),
                vmem((128, edges), F32),
                vmem((1, rows), F32),
                vmem((width, width), BF),
                vmem((BAND - 1, feat, rows), BF),
                vmem((BAND - 1, feat, rows), BF),
                vmem((width, width), F32),
                vmem((groups, feat, width), F32),
                vmem((rings, chunk, 128), F32),
                vmem((rings, chunk, 128), F32),
                vmem((chunk, 128), F32),
                vmem((spans, chunk, 128), F32),
                vmem((chunk, 128), F32),
                vmem((rings, chunk, 128), F32),
                pltpu.SemaphoreType.DMA((10, most)),
                pltpu.SemaphoreType.DMA((10, most)),
                pltpu.SemaphoreType.DMA((2, BAND - 1)),
                pltpu.SemaphoreType.DMA((2, BAND - 1)),
            ],
            compiler_params=pltpu.CompilerParams(
                collective_id=0, has_side_effects=True, vmem_limit_bytes=56 * 1024 * 1024
            ),
        )(feats, weight, words, mults, cotan)
    )


def solution(mesh, rings=RINGS):
    return jax.shard_map(
        functools.partial(body, rings),
        mesh=mesh,
        in_specs=(P("grp", "blk"), P(), P("grp", "blk"), P("grp", "blk"), P("grp", "blk")),
        out_specs=(P("grp", "blk"), P("grp", "blk"), P("grp", None)),
        check_vma=False,
    )
```

time: 772 us -> 112 us (0.15)
  blocking collectives: 344 us -> 0 us
  other arithmetic: 181 us -> 1.45 us
  waiting for transfers between devices: 158 us -> 0 us
  Pallas kernels: 0 us -> 105 us
  matrix products: 37.4 us -> 0 us
  starting transfers between devices: 35.9 us -> 0 us
  between operations: 14.3 us -> 0.69 us
    psum x1 -> x0, blocking collectives: 264 us -> none  [body(): grad_weight = lax.psum(weight_part, 'blk') * (rows_here * blocks) ** (-0.5)]
    reduce_sum x3 -> x0, other arithmetic: 177 us -> none  [the longest x2 177 us: adjacency(): jnp.sum(jnp.where(hits, masked[:, None, :], 0.0), axis=0)]
    pallas_call x0 -> x1, Pallas kernels: none -> 105 us  [body(): pl.pallas_call(functools.partial(kernel, (blocks, groups, rings)), out_sh...]
    reduce_scatter x1 -> x0, waiting for transfers between devices: 91 us -> none  [body(): lax.psum_scatter(lax.dot_general(w_rows, aggregated, (((0,), (0,)), ((),...]
    all_gather x2 -> x0, blocking collectives: 80.1 us -> none  [the longest x1 42.4 us: body(): weights_all = lax.all_gather(mult, 'grp', axis=0, tiled=True)]
    all_gather x1 -> x0, waiting for transfers between devices: 65.8 us -> none  [body(): grad_all = lax.all_gather(grad_z, 'grp', axis=0, tiled=True)]
    dot_general x11 -> x0, matrix products: 37.4 us -> none  [the longest x4 17.4 us: spread(): lax.dot_general(scaled_low, tiles[step], (((1,), (1,)), ((), ())), prefer...]
    ppermute x6 -> x0, starting transfers between devices: 35.8 us -> none  [shifted(): lax.ppermute(value, axis, [(i, (i + by) % devices) for i in range(devices)])]
  transfers between devices with their start and end apart: 8 -> 0, of which waited for: 4 -> 0; matrix products, arithmetic and copies ran while one was open for 25% -> 0% of each run, Pallas kernels for 0% -> 0%
where the time goes in v1:
time: 112 us; the launch traced here: 111 us
  Pallas kernels  105 us (94%)
  local copies, waits for them, and re-layouts  4.01 us (4%)
  other arithmetic  1.45 us (1%)
    pallas_call x1, Pallas kernels, body(): pl.pallas_call(functools.partial(kernel, (blocks, groups, rings)), out_sh...  105 us
    unnamed x11, local copies, waits for them, and re-layouts  3.11 us

profile of v1, /device:TPU:1, one launch (start us, length us, event | category | flops | bytes accessed | tf_op | source)
XLA Modules:
  0.0 111.4 jit_solution(14180026371365721324)
XLA Ops:
  0.6 0.0 copy-start.2
  0.6 0.8 fusion.1
  1.5 0.0 copy-done.2
  1.5 0.1 reshape.47
  1.6 0.7 copy.10
  2.3 0.1 reshape.45
  2.4 0.1 copy.12
  2.4 0.1 copy.11
  2.5 0.6 add_bitcast_fusion.words
  3.1 105.2 %shard_map.76 = (bf16[32,2048]{1,0:T(8,128)(2,1)}, f32[32,2048]{1,0:T(8,128)}, f32[32,256]{1,0:T(8,128)}) custom-call(bf16[32,2048]{1,0:T(8,128)(2,1)} %feats.1, bf16[256,256]{1,0:T(8,128)(2,1)} %weight.1, s32[16,128]{1,0:T(8,128)} %add_bitcast_fusion.words, bf16[2,16,128]{2,1,0:T(8,128)(2,1)} %bitcast.9, bf16[32,2048]{1,0:T(8,128)(2,1)} %cotan.1), custom_call_target="tpu_custom_call" | custom-call | tf_op jit(solution)/shard_map/pallas_call | solution.py:354
  108.4 0.0 copy-start
  108.4 1.6 %copy.16 = bf16[32,2048]{1,0:T(8,128)(2,1)} copy(bf16[32,2048]{1,0:T(8,128)(2,1)} %get-tuple-element.8) | data formatting | bytes 262144
  110.0 0.0 copy-done
  110.0 0.0 copy-start.1
  110.0 0.7 copy.17
  110.7 0.1 copy-done.1
  110.7 0.6 copy.18
  (1 shorter events, 0.0 us)
Async XLA Ops:
  0.6 0.8 copy-start.2
  108.4 1.6 %copy-start = (f32[32,2048]{1,0:T(8,128)S(1)}, f32[32,2048]{1,0:T(8,128)}, u32[]{:S(2)}) copy-start(f32[32,2048]{1,0:T(8,128)} %get-tuple-element.9) | copy-start | bytes 786436
  110.0 0.8 copy-start.1

commit v2 on v1

--- a/solution.py
+++ b/solution.py
@@ -14,19 +14,24 @@
 F32 = jnp.float32
 MESH = pl.DeviceIdType.MESH
 NT = (((1,), (1,)), ((), ()))
-WORDS, MULTS, COTS, AGGS, SGS, HIDS, GWS, RSUM, ZSUM, RALL = range(10)
+WORDS, MULTS, COTS, AGGS, SGS, HIDS, XSUM, RSUM, ZSUM, RALL = range(10)
+ZHI = 2
+PLANE = 16
+HI = 16
 
 
 def kernel(
     shape,
     feats,
     weight,
-    words,
-    mults,
+    nbr,
+    mult,
     cotan,
     hidden,
     grad_feats,
     grad_weight,
+    words,
+    mults,
     gw,
     gm,
     cot_all,
@@ -37,7 +42,9 @@
     sg,
     hid_own,
     adj,
-    e_lo,
+    spread,
+    e_lq,
+    e_lr,
     e_hi,
     e_m,
     root,
@@ -68,7 +75,10 @@
     core = lax.rem(b, CORES)
     ring = lax.rem(b // CORES, rings)
     z_lo = b // (CORES * rings)
-    span = z_lo * CORES + core
+    xs = groups // ZHI
+    z_hi = g // xs
+    x = lax.rem(g, xs)
+    span = (z_hi * spans + z_lo * CORES + core)
 
     def grp_dev(q):
         return (b, q)
@@ -76,8 +86,15 @@
     def ring_dev(q):
         return ((z_lo * rings + q) * CORES + core, g)
 
+    def x_dev(q):
+        return (b, z_hi * xs + q)
+
     def span_dev(q):
-        return (((q // CORES) * rings + ring) * CORES + lax.rem(q, CORES), g)
+        low = lax.rem(q, spans)
+        return (
+            ((low // CORES) * rings + ring) * CORES + lax.rem(low, CORES),
+            (q // spans) * xs + x,
+        )
 
     def rows_of(q):
         return pl.ds(pl.multiple_of(q * feat, feat), feat)
@@ -95,9 +112,9 @@
         AGGS: (grp_dev, g, groups, lambda q: agg_own.at[:, nodes_of(q)], lambda q: agg_all.at[rows_of(q), :]),
         SGS: (grp_dev, g, groups, lambda q: sg_own.at[rows_of(q), :], lambda q: sg.at[:, nodes_of(q)]),
         HIDS: (grp_dev, g, groups, lambda q: hid_own.at[rows_of(q), :], lambda q: hidden.at[:, nodes_of(q)]),
-        GWS: (grp_dev, g, groups, lambda q: gw_own.at[rows_of(q), :], lambda q: gw_in.at[q]),
+        XSUM: (x_dev, x, xs, lambda q: gw_own.at[:, q], lambda q: gw_in.at[q]),
         RSUM: (ring_dev, ring, rings, lambda q: t_own.at[q], lambda q: t_in.at[q]),
-        ZSUM: (span_dev, span, spans, lambda q: u_own, lambda q: u_in.at[q]),
+        ZSUM: (span_dev, span, ZHI * spans, lambda q: u_own.at[q // spans], lambda q: u_in.at[q]),
         RALL: (ring_dev, ring, rings, lambda q: v_own, lambda q: v_in.at[q]),
     }
 
@@ -169,66 +186,108 @@
     for off in range(1, BAND):
         greet((lax.rem(b + off, blocks), g))
         greet((lax.rem(b - off + blocks, blocks), g))
-    pl.semaphore_wait(barrier, groups - 1 + rings - 1 + spans - 1 + 2 * (BAND - 1))
+
+    pairs = nbr.shape[0] // 2
+    shift = rows.bit_length() - 1
+    code = nbr[...]
+    code = (((b - (code >> shift)) & (blocks - 1)) << shift) + (code & (rows - 1))
+    amounts = mult[...].astype(F32)
+
+    def plane(value, k):
+        return jnp.concatenate(
+            [value[k : k + 1, c * 128 : c * 128 + 128] for c in range(PLANE)], axis=0
+        )
+
+    for p in range(pairs):
+        at = pl.ds(p * PLANE, PLANE)
+        words[at, :] = plane(code, 2 * p) + (plane(code, 2 * p + 1) << 16)
+        for h in range(2):
+            mults[h, at, :] = plane(amounts, 2 * p + h).astype(BF)
+    pl.semaphore_wait(
+        barrier, groups - 1 + rings - 1 + ZHI * spans - 1 + 2 * (BAND - 1)
+    )
 
     send_all(WORDS)
     send_all(MULTS)
-    send_all(COTS)
     gw[edges_of(g), :] = words[...]
     gm[:, edges_of(g), :] = mults[...]
     cot_all[rows_of(g), :] = cotan[:, nodes_of(g)]
     w_t[...] = weight[...].astype(F32).T.astype(BF)
-    wait_all(WORDS)
+    edges = 256
+    lane_e = lax.broadcasted_iota(jnp.int32, (128, edges), 1)
+    row_l = lax.broadcasted_iota(jnp.int32, (128, edges), 0)
+    folds = (lane_e & 15) == (row_l & 15)
+    for k in range(16):
+        spread[k * 128 : k * 128 + 128, :] = jnp.where(
+            folds & ((lane_e >> 4) == k), 1.0, 0.0
+        ).astype(BF)
     wait_all(MULTS)
 
-    half = gw.shape[0]
+    planes = gw.shape[0] // PLANE
+    line = jnp.zeros((PLANE, 128), F32)
     for h in range(2):
-        code = (gw[...] >> (16 * h)) & 0xFFFF
-        at = pl.ds(h * half, half)
-        e_lo[:, at] = (code & 255).astype(F32).T
-        e_hi[:, at] = (code >> 8).astype(F32).T
-        e_m[:, at] = gm[h].astype(F32).T
-    edges = 2 * half
-    fold = (
-        lax.rem(lax.broadcasted_iota(jnp.int32, (edges, 128), 0), 16)
-        == lax.rem(lax.broadcasted_iota(jnp.int32, (edges, 128), 1), 16)
-    )
-    fold = jnp.where(fold, 1.0, 0.0).astype(BF)
-    degree = jnp.dot(e_m[...].astype(BF), fold, preferred_element_type=F32)
-    pick = (
-        lax.broadcasted_iota(jnp.int32, (8, 128), 0)
-        == lax.broadcasted_iota(jnp.int32, (8, 128), 1) // 16
-    )
-    for c in range(rows // 128):
-        line = jnp.sum(jnp.where(pick, degree[c * 8 : c * 8 + 8, :], 0.0), axis=0, keepdims=True)
-        root[:, c * 128 : c * 128 + 128] = lax.rsqrt(1.0 + line)
+        for q in range(planes):
+            line = line + gm[h, q * PLANE : q * PLANE + PLANE, :].astype(F32)
+    line = lax.rsqrt(1.0 + line)
+    for c in range(PLANE):
+        root[:, c * 128 : c * 128 + 128] = line[c : c + 1, :]
     halo[:, pl.ds(0, rows)] = (feats[...].astype(F32) * root[...]).astype(BF)
     for off in range(1, BAND):
         halo_copy(off).start()
-
-    hi_count = BAND * rows // 256
+    send_all(COTS)
+    wait_all(WORDS)
+
+    seat = (
+        lax.broadcasted_iota(jnp.int32, (PLANE, 8, 128), 2) >> 4
+    ) == lax.broadcasted_iota(jnp.int32, (PLANE, 8, 128), 1)
+
+    def seated(value):
+        wide = jnp.broadcast_to(value.astype(F32)[:, None, :], (PLANE, 8, 128))
+        return jnp.where(seat, wide, 0.0).reshape(PLANE * 8, 128).astype(BF)
+
+    def table(pick):
+        wide = jnp.concatenate(
+            [seated(pick(h, pl.ds(q * PLANE, PLANE))) for h in range(2) for q in range(planes)],
+            axis=1,
+        )
+        return jnp.dot(wide, spread[...], preferred_element_type=F32)
+
+    def field(low, mask):
+        return lambda h, at: (gw[at, :] >> (16 * h + low)) & mask
+
+    e_lr[...] = table(field(0, 15))
+    e_lq[...] = table(field(4, 31))
+    e_hi[...] = table(field(9, 15))
+    e_m[...] = table(lambda h, at: gm[h, at, :])
+
+    lo_chunks = BAND * rows // HI // 16
     sub = lax.broadcasted_iota(jnp.int32, (16, edges), 0)
-    own_lane = lax.rem(lax.broadcasted_iota(jnp.int32, (16, edges), 1), 16) == sub
+    own_lane = (lax.broadcasted_iota(jnp.int32, (16, edges), 1) & 15) == sub
     sub_f = sub.astype(F32)
-
-    @pl.loop(0, rows // 16)
+    zero = jnp.zeros((16, edges), BF)
+    ones = jnp.ones((16, edges), BF)
+
+    @pl.loop(0, rows // 16, unroll=8)
     def _(t):
         one = pl.ds(t, 1)
-        low = (jnp.broadcast_to(e_lo[one, :], (16, edges)) - sub_f).astype(BF)
-        high = jnp.broadcast_to(e_hi[one, :], (16, edges)).astype(BF)
-        amount = jnp.where(own_lane, jnp.broadcast_to(e_m[one, :], (16, edges)), 0.0).astype(BF)
-        zero = jnp.zeros((16, edges), BF)
-        ones = jnp.ones((16, edges), BF)
+
+        def row(ref):
+            return jnp.broadcast_to(ref[one, :], (16, edges))
+
+        low = jnp.where(row(e_lr) == sub_f, row(e_lq), -1.0).astype(BF)
+        high = row(e_hi).astype(BF)
+        amount = jnp.where(own_lane, row(e_m), 0.0).astype(BF)
         right = jnp.concatenate(
-            [jnp.where(low == jnp.asarray(16.0 * c, BF), ones, zero) for c in range(16)], axis=0
+            [jnp.where(low == jnp.asarray(float(c), BF), ones, zero) for c in range(lo_chunks)],
+            axis=0,
         )
         left = jnp.concatenate(
-            [jnp.where(high == jnp.asarray(float(c), BF), amount, zero) for c in range(hi_count)],
+            [jnp.where(high == jnp.asarray(float(c), BF), amount, zero) for c in range(HI)],
             axis=0,
         )
         made = lax.dot_general(left, right, NT, preferred_element_type=F32).astype(BF)
         adj[pl.ds(pl.multiple_of(t * 16, 16), 16), :] = jnp.concatenate(
-            [made[c * 16 : c * 16 + 16, :] for c in range(hi_count)], axis=1
+            [made[c * 16 : c * 16 + 16, :] for c in range(HI)], axis=1
         )
 
     for off in range(1, BAND):
@@ -261,12 +320,14 @@
     grad_agg = jnp.dot(weight[...], grad_z, preferred_element_type=F32)
     sg_own[...] = (root[:, nodes_of(g)] * grad_agg).astype(BF)
     send_all(SGS)
-    gw_own[...] = lax.dot_general(agg_all[...], grad_z, NT, preferred_element_type=F32)
-    send_all(GWS)
+    product = lax.dot_general(agg_all[...], grad_z, NT, preferred_element_type=F32)
+    for q in range(groups):
+        gw_own[q // xs, q % xs] = product[q * feat : q * feat + feat, :]
+    send_all(XSUM)
     hid_own[...] = (z * s).astype(BF)
     send_all(HIDS)
     sg[:, nodes_of(g)] = sg_own[rows_of(g), :]
-    gw_in[g] = gw_own[rows_of(g), :]
+    gw_in[x] = gw_own[:, x]
     hidden[:, nodes_of(g)] = hid_own[rows_of(g), :]
     wait_all(SGS)
 
@@ -286,13 +347,13 @@
         if off > 0:
             back_copy(off).start()
         if off == 3:
-            wait_all(GWS)
+            wait_all(XSUM)
             total = gw_in[0]
-            for q in range(1, groups):
+            for q in range(1, xs):
                 total = total + gw_in[q]
             for q in range(rings):
                 t_own[q] = total[
-                    (q // 2) * chunk : (q // 2 + 1) * chunk, (q % 2) * 128 : (q % 2) * 128 + 128
+                    :, (q // 2) * chunk : (q // 2 + 1) * chunk, (q % 2) * 128 : (q % 2) * 128 + 128
                 ]
             send_all(RSUM)
             t_in[ring] = t_own[ring]
@@ -303,11 +364,11 @@
                 total = total + t_in[q]
             u_own[...] = total
             send_all(ZSUM)
-            u_in[span] = u_own[...]
+            u_in[span] = u_own[z_hi]
         elif off == 1:
             wait_all(ZSUM)
             total = u_in[0]
-            for q in range(1, spans):
+            for q in range(1, ZHI * spans):
                 total = total + u_in[q]
             v_own[...] = total * (rows * blocks) ** (-0.5)
             send_all(RALL)
@@ -332,6 +393,15 @@
         back_copy(off).wait_send()
 
 
+def settle(*refs):
+    sems = refs[6]
+    copies = [pltpu.make_async_copy(refs[i], refs[3 + i], sems.at[i]) for i in range(3)]
+    for copy in copies:
+        copy.start()
+    for copy in copies:
+        copy.wait()
+
+
 def body(rings, feats, weight, nbr, mult, cotan):
     feat, rows = feats.shape
     slots = nbr.shape[0]
@@ -339,19 +409,12 @@
     groups = lax.axis_size("grp")
     width = feat * groups
     slice_n = rows // groups
-    b = lax.axis_index("blk")
-    code = ((b - nbr // rows + blocks) % blocks) * rows + nbr % rows
-    code = code.reshape(slots // 2, 2, rows // 16, 16)
-    words = (code[:, 0] + code[:, 1] * 65536).transpose(0, 2, 1).reshape(slots * 8, rows // 16)
-    mults = mult.reshape(slots // 2, 2, rows // 16, 16).transpose(1, 0, 3, 2)
-    mults = mults.reshape(2, slots * 8, rows // 16)
     chunk = feat // (rings // 2)
     spans = blocks // rings
     vmem = pltpu.VMEM
     edges = 256
-    most = max(groups, rings, spans)
-    return tuple(
-        pl.pallas_call(
+    most = max(groups, rings, ZHI * spans)
+    outs = pl.pallas_call(
             functools.partial(kernel, (blocks, groups, rings)),
             out_shape=(
                 jax.ShapeDtypeStruct((feat, rows), BF),
@@ -361,6 +424,8 @@
             in_specs=[pl.BlockSpec(memory_space=vmem)] * 5,
             out_specs=(pl.BlockSpec(memory_space=vmem),) * 3,
             scratch_shapes=[
+                vmem((slots * 8, 128), jnp.int32),
+                vmem((2, slots * 8, 128), BF),
                 vmem((edges // 2, 128), jnp.int32),
                 vmem((2, edges // 2, 128), BF),
                 vmem((width, slice_n), BF),
@@ -371,6 +436,8 @@
                 vmem((feat, rows), BF),
                 vmem((width, slice_n), BF),
                 vmem((rows, BAND * rows), BF),
+                vmem((16 * 128, edges), BF),
+                vmem((128, edges), F32),
                 vmem((128, edges), F32),
                 vmem((128, edges), F32),
                 vmem((128, edges), F32),
@@ -378,12 +445,12 @@
                 vmem((width, width), BF),
                 vmem((BAND - 1, feat, rows), BF),
                 vmem((BAND - 1, feat, rows), BF),
-                vmem((width, width), F32),
-                vmem((groups, feat, width), F32),
-                vmem((rings, chunk, 128), F32),
-                vmem((rings, chunk, 128), F32),
-                vmem((chunk, 128), F32),
-                vmem((spans, chunk, 128), F32),
+                vmem((ZHI, groups // ZHI, feat, width), F32),
+                vmem((groups // ZHI, ZHI, feat, width), F32),
+                vmem((rings, ZHI, chunk, 128), F32),
+                vmem((rings, ZHI, chunk, 128), F32),
+                vmem((ZHI, chunk, 128), F32),
+                vmem((ZHI * spans, chunk, 128), F32),
                 vmem((chunk, 128), F32),
                 vmem((rings, chunk, 128), F32),
                 pltpu.SemaphoreType.DMA((10, most)),
@@ -392,9 +459,17 @@
                 pltpu.SemaphoreType.DMA((2, BAND - 1)),
             ],
             compiler_params=pltpu.CompilerParams(
-                collective_id=0, has_side_effects=True, vmem_limit_bytes=56 * 1024 * 1024
+                collective_id=0, has_side_effects=True, vmem_limit_bytes=46 * 1024 * 1024
             ),
-        )(feats, weight, words, mults, cotan)
+        )(feats, weight, nbr, mult, cotan)
+    return tuple(
+        pl.pallas_call(
+            settle,
+            out_shape=[jax.ShapeDtypeStruct(o.shape, o.dtype) for o in outs],
+            in_specs=[pl.BlockSpec(memory_space=pl.ANY)] * 3,
+            out_specs=[pl.BlockSpec(memory_space=pl.ANY)] * 3,
+            scratch_shapes=[pltpu.SemaphoreType.DMA((3,))],
+        )(*outs)
     )
 
 

time: 112 us -> 101 us (0.902)
  Pallas kernels: 105 us -> 94.4 us
  local copies, waits for them, and re-layouts: 4.01 us -> 6.06 us
  other arithmetic: 1.45 us -> 0 us
    pallas_call x1, Pallas kernels: 105 us -> 80.3 us  [body(): pl.pallas_call(functools.partial(kernel, (blocks, groups, rings)), out_sh...]
    pallas_call x0 -> x1, Pallas kernels: none -> 14 us  [body(): pl.pallas_call(settle, out_shape=[jax.ShapeDtypeStruct(o.shape, o.dtype)...]
    unnamed x11 -> x16, local copies, waits for them, and re-layouts: 3.11 us -> 6.06 us
where the time goes in v2:
time: 101 us
  Pallas kernels  94.4 us (93%)
  local copies, waits for them, and re-layouts  6.06 us (6%)
    pallas_call x1, Pallas kernels, body(): pl.pallas_call(functools.partial(kernel, (blocks, groups, rings)), out_sh...  80.3 us
    pallas_call x1, Pallas kernels, body(): pl.pallas_call(settle, out_shape=[jax.ShapeDtypeStruct(o.shape, o.dtype)...  14 us
    unnamed x16, local copies, waits for them, and re-layouts  6.06 us

profile of v2, /device:TPU:1, one launch (start us, length us, event | category | flops | bytes accessed | tf_op | source)
XLA Modules:
  0.0 101.1 jit_solution(6187031797967087291)
XLA Ops:
  0.6 0.0 copy-start.1
  0.6 0.9 copy-done.1
  1.5 0.0 copy-start.2
  1.5 0.9 copy-done.2
  2.4 0.0 copy-start.3
  2.4 0.9 copy-done.3
  3.3 0.0 copy-start.6
  3.3 0.7 copy-done.6
  4.1 0.0 copy-start.7
  4.1 0.7 copy-done.7
  4.8 80.3 %shard_map.76 = (bf16[32,2048]{1,0:T(8,128)(2,1)S(1)}, f32[32,2048]{1,0:T(8,128)S(1)}, f32[32,256]{1,0:T(8,128)S(1)}) custom-call(bf16[32,2048]{1,0:T(8,128)(2,1)S(1)} %copy-done.1, bf16[256,256]{1,0:T(8,128)(2,1)S(1)} %copy-done.2, s32[2,2048]{1,0:T(2,128)S(1)} %copy-done.6, bf16[2,2048]{1,0:T(2,128)(2,1)S(1)} %copy-done.7, bf16[32,2048]{1,0:T(8,128)(2,1)S(1)} %copy-done.3), custom_call_target="tpu_custom_call" | custom-call | tf_op jit(solution)/shard_map/pallas_call | solution.py:417
  85.1 0.0 copy-start
  85.1 0.7 copy-done
  85.8 0.0 copy-start.4
  85.8 0.6 copy-done.4
  86.4 0.0 copy-start.5
  86.4 0.6 copy-done.5
  87.1 14.0 %shard_map.77 = (bf16[32,2048]{1,0:T(8,128)(2,1)}, f32[32,2048]{1,0:T(8,128)}, f32[32,256]{1,0:T(8,128)}) custom-call(bf16[32,2048]{1,0:T(8,128)(2,1)} %copy-done.4, f32[32,2048]{1,0:T(8,128)} %copy-done, f32[32,256]{1,0:T(8,128)} %copy-done.5), custom_call_target="tpu_custom_call" | custom-call | tf_op jit(solution)/shard_map/pallas_call | solution.py:466
Async XLA Ops:
  0.6 0.9 copy-start.1
  1.5 0.9 copy-start.2
  2.4 0.9 copy-start.3
  3.3 0.7 copy-start.6
  4.1 0.7 copy-start.7
  85.1 0.7 copy-start
  85.8 0.6 copy-start.4
  86.4 0.6 copy-start.5

commit v3 on v2

--- a/solution.py
+++ b/solution.py
@@ -22,11 +22,11 @@
 
 def kernel(
     shape,
-    feats,
-    weight,
+    feats_in,
+    weight_in,
     nbr,
     mult,
-    cotan,
+    cotan_in,
     hidden,
     grad_feats,
     grad_weight,
@@ -63,6 +63,10 @@
     recv_sem,
     hsend,
     hrecv,
+    feats,
+    weight,
+    cotan,
+    load_sem,
 ):
     blocks, groups, rings = shape
     feat, rows = feats.shape
@@ -176,6 +180,14 @@
             device_id_type=MESH,
         )
 
+    loads = [
+        pltpu.make_async_copy(here, there, load_sem.at[i])
+        for i, (here, there) in enumerate(
+            ((feats_in, feats), (weight_in, weight), (cotan_in, cotan))
+        )
+    ]
+    for load in loads:
+        load.start()
     barrier = pltpu.get_barrier_semaphore()
 
     def greet(dev):
@@ -203,6 +215,8 @@
         words[at, :] = plane(code, 2 * p) + (plane(code, 2 * p + 1) << 16)
         for h in range(2):
             mults[h, at, :] = plane(amounts, 2 * p + h).astype(BF)
+    for load in loads:
+        load.wait()
     pl.semaphore_wait(
         barrier, groups - 1 + rings - 1 + ZHI * spans - 1 + 2 * (BAND - 1)
     )
@@ -322,42 +336,40 @@
     send_all(SGS)
     product = lax.dot_general(agg_all[...], grad_z, NT, preferred_element_type=F32)
     for q in range(groups):
-        gw_own[q // xs, q % xs] = product[q * feat : q * feat + feat, :]
+        gw_own[q // xs, q % xs] = product[q * feat : q * feat + feat, :].astype(BF)
     send_all(XSUM)
     hid_own[...] = (z * s).astype(BF)
-    send_all(HIDS)
     sg[:, nodes_of(g)] = sg_own[rows_of(g), :]
     gw_in[x] = gw_own[:, x]
     hidden[:, nodes_of(g)] = hid_own[rows_of(g), :]
+
+    chunk = feat // (rings // 2)
+    wait_all(XSUM)
+    total = gw_in[0].astype(F32)
+    for q in range(1, xs):
+        total = total + gw_in[q].astype(F32)
+    for q in range(rings):
+        t_own[q] = total[
+            :, (q // 2) * chunk : (q // 2 + 1) * chunk, (q % 2) * 128 : (q % 2) * 128 + 128
+        ]
+    send_all(RSUM)
+    t_in[ring] = t_own[ring]
+    send_all(HIDS)
     wait_all(SGS)
 
-    chunk = feat // (rings // 2)
     for off in range(BAND - 1, -1, -1):
 
-        @pl.loop(0, rows // 256)
-        def _(i, off=off):
-            at = pl.ds(pl.multiple_of(i * 256, 256), 256)
-            src = pl.ds(pl.multiple_of(off * rows + i * 256, 256), 256)
-            value = jnp.dot(sg[...], adj[:, src], preferred_element_type=F32)
-            if off > 0:
-                part[off - 1, :, at] = value.astype(BF)
-            else:
-                grad_feats[:, at] = value + sg[:, at].astype(F32)
+        value = jnp.dot(
+            sg[...], adj[:, pl.ds(off * rows, rows)], preferred_element_type=F32
+        )
+        if off > 0:
+            part[off - 1] = value.astype(BF)
+        else:
+            grad_feats[...] = value + sg[...].astype(F32)
 
         if off > 0:
             back_copy(off).start()
-        if off == 3:
-            wait_all(XSUM)
-            total = gw_in[0]
-            for q in range(1, xs):
-                total = total + gw_in[q]
-            for q in range(rings):
-                t_own[q] = total[
-                    :, (q // 2) * chunk : (q // 2 + 1) * chunk, (q % 2) * 128 : (q % 2) * 128 + 128
-                ]
-            send_all(RSUM)
-            t_in[ring] = t_own[ring]
-        elif off == 2:
+        if off == 2:
             wait_all(RSUM)
             total = t_in[0]
             for q in range(1, rings):
@@ -365,20 +377,14 @@
             u_own[...] = total
             send_all(ZSUM)
             u_in[span] = u_own[z_hi]
-        elif off == 1:
-            wait_all(ZSUM)
-            total = u_in[0]
-            for q in range(1, ZHI * spans):
-                total = total + u_in[q]
-            v_own[...] = total * (rows * blocks) ** (-0.5)
-            send_all(RALL)
-            v_in[ring] = v_own[...]
-
-    wait_all(RALL)
-    for q in range(rings):
-        grad_weight[
-            (q // 2) * chunk : (q // 2 + 1) * chunk, (q % 2) * 128 : (q % 2) * 128 + 128
-        ] = v_in[q]
+
+    wait_all(ZSUM)
+    total = u_in[0]
+    for q in range(1, ZHI * spans):
+        total = total + u_in[q]
+    v_own[...] = total * (rows * blocks) ** (-0.5)
+    send_all(RALL)
+    v_in[ring] = v_own[...]
     for off in range(1, BAND):
         back_copy(off).wait_recv()
     carried = arrived[0].astype(F32)
@@ -386,6 +392,11 @@
         carried = carried + arrived[off - 1].astype(F32)
     grad_feats[...] = root[...] * (grad_feats[...] + carried)
     wait_all(HIDS)
+    wait_all(RALL)
+    for q in range(rings):
+        grad_weight[
+            (q // 2) * chunk : (q // 2 + 1) * chunk, (q % 2) * 128 : (q % 2) * 128 + 128
+        ] = v_in[q]
     for phase in plans:
         sent_all(phase)
     for off in range(1, BAND):
@@ -394,11 +405,15 @@
 
 
 def settle(*refs):
-    sems = refs[6]
-    copies = [pltpu.make_async_copy(refs[i], refs[3 + i], sems.at[i]) for i in range(3)]
-    for copy in copies:
+    kept, sems = refs[6:9], refs[9]
+    arrive = [pltpu.make_async_copy(refs[i], kept[i], sems.at[0, i]) for i in range(3)]
+    leave = [pltpu.make_async_copy(kept[i], refs[3 + i], sems.at[1, i]) for i in range(3)]
+    for copy in arrive:
         copy.start()
-    for copy in copies:
+    for i in (2, 0, 1):
+        arrive[i].wait()
+        leave[i].start()
+    for copy in leave:
         copy.wait()
 
 
@@ -421,7 +436,9 @@
                 jax.ShapeDtypeStruct((feat, rows), F32),
                 jax.ShapeDtypeStruct((feat, width), F32),
             ),
-            in_specs=[pl.BlockSpec(memory_space=vmem)] * 5,
+            in_specs=[
+                pl.BlockSpec(memory_space=pl.ANY if i in (0, 1, 4) else vmem) for i in range(5)
+            ],
             out_specs=(pl.BlockSpec(memory_space=vmem),) * 3,
             scratch_shapes=[
                 vmem((slots * 8, 128), jnp.int32),
@@ -445,8 +462,8 @@
                 vmem((width, width), BF),
                 vmem((BAND - 1, feat, rows), BF),
                 vmem((BAND - 1, feat, rows), BF),
-                vmem((ZHI, groups // ZHI, feat, width), F32),
-                vmem((groups // ZHI, ZHI, feat, width), F32),
+                vmem((ZHI, groups // ZHI, feat, width), BF),
+                vmem((groups // ZHI, ZHI, feat, width), BF),
                 vmem((rings, ZHI, chunk, 128), F32),
                 vmem((rings, ZHI, chunk, 128), F32),
                 vmem((ZHI, chunk, 128), F32),
@@ -457,9 +474,13 @@
                 pltpu.SemaphoreType.DMA((10, most)),
                 pltpu.SemaphoreType.DMA((2, BAND - 1)),
                 pltpu.SemaphoreType.DMA((2, BAND - 1)),
+                vmem((feat, rows), BF),
+                vmem((width, width), BF),
+                vmem((feat, rows), BF),
+                pltpu.SemaphoreType.DMA((3,)),
             ],
             compiler_params=pltpu.CompilerParams(
-                collective_id=0, has_side_effects=True, vmem_limit_bytes=46 * 1024 * 1024
+                collective_id=0, has_side_effects=True, vmem_limit_bytes=60 * 1024 * 1024
             ),
         )(feats, weight, nbr, mult, cotan)
     return tuple(
@@ -468,7 +489,9 @@
             out_shape=[jax.ShapeDtypeStruct(o.shape, o.dtype) for o in outs],
             in_specs=[pl.BlockSpec(memory_space=pl.ANY)] * 3,
             out_specs=[pl.BlockSpec(memory_space=pl.ANY)] * 3,
-            scratch_shapes=[pltpu.SemaphoreType.DMA((3,))],
+            scratch_shapes=[pltpu.VMEM(o.shape, o.dtype) for o in outs]
+            + [pltpu.SemaphoreType.DMA((2, 3))],
+            compiler_params=pltpu.CompilerParams(vmem_limit_bytes=60 * 1024 * 1024),
         )(*outs)
     )
 

time: 101 us -> 78.7 us (0.78)
  Pallas kernels: 94.4 us -> 77.8 us
  local copies, waits for them, and re-layouts: 6.06 us -> 0 us
    pallas_call x1, Pallas kernels: 14 us -> 1.78 us  [body(): pl.pallas_call(settle, out_shape=[jax.ShapeDtypeStruct(o.shape, o.dtype)...]
    unnamed x16 -> x0, local copies, waits for them, and re-layouts: 6.06 us -> none
    pallas_call x1, Pallas kernels: 80.3 us -> 76 us  [body(): pl.pallas_call(functools.partial(kernel, (blocks, groups, rings)), out_sh...]
where the time goes in v3:
time: 78.7 us; the launch traced here: 78.4 us
  Pallas kernels  77.8 us (99%)
    pallas_call x1, Pallas kernels, body(): pl.pallas_call(functools.partial(kernel, (blocks, groups, rings)), out_sh...  76 us
    pallas_call x1, Pallas kernels, body(): pl.pallas_call(settle, out_shape=[jax.ShapeDtypeStruct(o.shape, o.dtype)...  1.78 us

profile of v3, /device:TPU:1, one launch (start us, length us, event | category | flops | bytes accessed | tf_op | source)
XLA Modules:
  0.0 78.4 jit_solution(4245756239555396536)
XLA Ops:
  0.6 76.0 %shard_map.76 = (bf16[32,2048]{1,0:T(8,128)(2,1)}, f32[32,2048]{1,0:T(8,128)}, f32[32,256]{1,0:T(8,128)}) custom-call(bf16[32,2048]{1,0:T(8,128)(2,1)} %feats_in.1, bf16[256,256]{1,0:T(8,128)(2,1)} %weight_in.1, s32[2,2048]{1,0:T(2,128)} %nbr.1, bf16[2,2048]{1,0:T(2,128)(2,1)} %mult.1, bf16[32,2048]{1,0:T(8,128)(2,1)} %cotan_in.1), custom_call_target="tpu_custom_call" | custom-call | tf_op jit(solution)/shard_map/pallas_call | solution.py:432
  76.6 1.8 %shard_map.77 = (bf16[32,2048]{1,0:T(8,128)(2,1)}, f32[32,2048]{1,0:T(8,128)}, f32[32,256]{1,0:T(8,128)}) custom-call(bf16[32,2048]{1,0:T(8,128)(2,1)} %get-tuple-element.6.refs_0_, f32[32,2048]{1,0:T(8,128)} %get-tuple-element.7.refs_1_, f32[32,256]{1,0:T(8,128)} %get-tuple-element.8.refs_2_), custom_call_target="tpu_custom_call" | custom-call | tf_op jit(solution)/shard_map/pallas_call | solution.py:487

commit v4 on v3

--- a/solution.py
+++ b/solution.py
@@ -14,7 +14,7 @@
 F32 = jnp.float32
 MESH = pl.DeviceIdType.MESH
 NT = (((1,), (1,)), ((), ()))
-WORDS, MULTS, COTS, AGGS, SGS, HIDS, XSUM, RSUM, ZSUM, RALL = range(10)
+WORDS, MULTS, COTS, AGGS, SGS, HIDS, RSUM, ZSUM, RALL = range(9)
 ZHI = 2
 PLANE = 16
 HI = 16
@@ -51,8 +51,6 @@
     w_t,
     part,
     arrived,
-    gw_own,
-    gw_in,
     t_own,
     t_in,
     u_own,
@@ -90,8 +88,11 @@
     def ring_dev(q):
         return ((z_lo * rings + q) * CORES + core, g)
 
-    def x_dev(q):
-        return (b, z_hi * xs + q)
+    def plane_dev(q):
+        return (
+            (z_lo * rings + lax.rem(q, rings)) * CORES + core,
+            z_hi * xs + q // rings,
+        )
 
     def span_dev(q):
         low = lax.rem(q, spans)
@@ -116,8 +117,7 @@
         AGGS: (grp_dev, g, groups, lambda q: agg_own.at[:, nodes_of(q)], lambda q: agg_all.at[rows_of(q), :]),
         SGS: (grp_dev, g, groups, lambda q: sg_own.at[rows_of(q), :], lambda q: sg.at[:, nodes_of(q)]),
         HIDS: (grp_dev, g, groups, lambda q: hid_own.at[rows_of(q), :], lambda q: hidden.at[:, nodes_of(q)]),
-        XSUM: (x_dev, x, xs, lambda q: gw_own.at[:, q], lambda q: gw_in.at[q]),
-        RSUM: (ring_dev, ring, rings, lambda q: t_own.at[q], lambda q: t_in.at[q]),
+        RSUM: (plane_dev, x * rings + ring, xs * rings, lambda q: t_own.at[q], lambda q: t_in.at[q]),
         ZSUM: (span_dev, span, ZHI * spans, lambda q: u_own.at[q // spans], lambda q: u_in.at[q]),
         RALL: (ring_dev, ring, rings, lambda q: v_own, lambda q: v_in.at[q]),
     }
@@ -218,7 +218,7 @@
     for load in loads:
         load.wait()
     pl.semaphore_wait(
-        barrier, groups - 1 + rings - 1 + ZHI * spans - 1 + 2 * (BAND - 1)
+        barrier, groups - 1 + xs * rings - 1 + ZHI * spans - 1 + 2 * (BAND - 1)
     )
 
     send_all(WORDS)
@@ -281,7 +281,7 @@
     zero = jnp.zeros((16, edges), BF)
     ones = jnp.ones((16, edges), BF)
 
-    @pl.loop(0, rows // 16, unroll=8)
+    @pl.loop(0, rows // 16, unroll=32)
     def _(t):
         one = pl.ds(t, 1)
 
@@ -335,25 +335,19 @@
     sg_own[...] = (root[:, nodes_of(g)] * grad_agg).astype(BF)
     send_all(SGS)
     product = lax.dot_general(agg_all[...], grad_z, NT, preferred_element_type=F32)
-    for q in range(groups):
-        gw_own[q // xs, q % xs] = product[q * feat : q * feat + feat, :].astype(BF)
-    send_all(XSUM)
+    chunk = feat // (rings // 2)
+    for q in range(xs * rings):
+        for h in range(ZHI):
+            top = (h * xs + q // rings) * feat + (q % rings // 2) * chunk
+            t_own[q, h * chunk : h * chunk + chunk, :] = product[
+                top : top + chunk, (q % 2) * 128 : (q % 2) * 128 + 128
+            ].astype(BF)
+    send_all(RSUM)
+    t_in[x * rings + ring] = t_own[x * rings + ring]
     hid_own[...] = (z * s).astype(BF)
     sg[:, nodes_of(g)] = sg_own[rows_of(g), :]
-    gw_in[x] = gw_own[:, x]
     hidden[:, nodes_of(g)] = hid_own[rows_of(g), :]
 
-    chunk = feat // (rings // 2)
-    wait_all(XSUM)
-    total = gw_in[0].astype(F32)
-    for q in range(1, xs):
-        total = total + gw_in[q].astype(F32)
-    for q in range(rings):
-        t_own[q] = total[
-            :, (q // 2) * chunk : (q // 2 + 1) * chunk, (q % 2) * 128 : (q % 2) * 128 + 128
-        ]
-    send_all(RSUM)
-    t_in[ring] = t_own[ring]
     send_all(HIDS)
     wait_all(SGS)
 
@@ -369,12 +363,13 @@
 
         if off > 0:
             back_copy(off).start()
-        if off == 2:
+        if off == 3:
             wait_all(RSUM)
-            total = t_in[0]
-            for q in range(1, rings):
-                total = total + t_in[q]
-            u_own[...] = total
+            total = t_in[0].astype(F32)
+            for q in range(1, xs * rings):
+                total = total + t_in[q].astype(F32)
+            for h in range(ZHI):
+                u_own[h] = total[h * chunk : h * chunk + chunk]
             send_all(ZSUM)
             u_in[span] = u_own[z_hi]
 
@@ -428,7 +423,7 @@
     spans = blocks // rings
     vmem = pltpu.VMEM
     edges = 256
-    most = max(groups, rings, ZHI * spans)
+    most = max(groups, rings * groups // ZHI, ZHI * spans)
     outs = pl.pallas_call(
             functools.partial(kernel, (blocks, groups, rings)),
             out_shape=(
@@ -462,16 +457,14 @@
                 vmem((width, width), BF),
                 vmem((BAND - 1, feat, rows), BF),
                 vmem((BAND - 1, feat, rows), BF),
-                vmem((ZHI, groups // ZHI, feat, width), BF),
-                vmem((groups // ZHI, ZHI, feat, width), BF),
-                vmem((rings, ZHI, chunk, 128), F32),
-                vmem((rings, ZHI, chunk, 128), F32),
+                vmem((rings * groups // ZHI, ZHI * chunk, 128), BF),
+                vmem((rings * groups // ZHI, ZHI * chunk, 128), BF),
                 vmem((ZHI, chunk, 128), F32),
                 vmem((ZHI * spans, chunk, 128), F32),
                 vmem((chunk, 128), F32),
                 vmem((rings, chunk, 128), F32),
-                pltpu.SemaphoreType.DMA((10, most)),
-                pltpu.SemaphoreType.DMA((10, most)),
+                pltpu.SemaphoreType.DMA((9, most)),
+                pltpu.SemaphoreType.DMA((9, most)),
                 pltpu.SemaphoreType.DMA((2, BAND - 1)),
                 pltpu.SemaphoreType.DMA((2, BAND - 1)),
                 vmem((feat, rows), BF),

time: 78.7 us -> 78.4 us (level)
  no operation moved by 1% of the time
where the time goes in v4:
time: 78.4 us; the launch traced here: 78.1 us
  Pallas kernels  77.5 us (99%)
    pallas_call x1, Pallas kernels, body(): pl.pallas_call(functools.partial(kernel, (blocks, groups, rings)), out_sh...  75.7 us
    pallas_call x1, Pallas kernels, body(): pl.pallas_call(settle, out_shape=[jax.ShapeDtypeStruct(o.shape, o.dtype)...  1.78 us

profile of v4, /device:TPU:1, one launch (start us, length us, event | category | flops | bytes accessed | tf_op | source)
XLA Modules:
  0.0 78.1 jit_solution(978765789308085127)
XLA Ops:
  0.6 75.7 %shard_map.76 = (bf16[32,2048]{1,0:T(8,128)(2,1)}, f32[32,2048]{1,0:T(8,128)}, f32[32,256]{1,0:T(8,128)}) custom-call(bf16[32,2048]{1,0:T(8,128)(2,1)} %feats_in.1, bf16[256,256]{1,0:T(8,128)(2,1)} %weight_in.1, s32[2,2048]{1,0:T(2,128)} %nbr.1, bf16[2,2048]{1,0:T(2,128)(2,1)} %mult.1, bf16[32,2048]{1,0:T(8,128)(2,1)} %cotan_in.1), custom_call_target="tpu_custom_call" | custom-call | tf_op jit(solution)/shard_map/pallas_call | solution.py:427
  76.3 1.8 %shard_map.77 = (bf16[32,2048]{1,0:T(8,128)(2,1)}, f32[32,2048]{1,0:T(8,128)}, f32[32,256]{1,0:T(8,128)}) custom-call(bf16[32,2048]{1,0:T(8,128)(2,1)} %get-tuple-element.6.refs_0_, f32[32,2048]{1,0:T(8,128)} %get-tuple-element.7.refs_1_, f32[32,256]{1,0:T(8,128)} %get-tuple-element.8.refs_2_), custom_call_target="tpu_custom_call" | custom-call | tf_op jit(solution)/shard_map/pallas_call | solution.py:480

commit v5 on v4

--- a/solution.py
+++ b/solution.py
@@ -281,7 +281,7 @@
     zero = jnp.zeros((16, edges), BF)
     ones = jnp.ones((16, edges), BF)
 
-    @pl.loop(0, rows // 16, unroll=32)
+    @pl.loop(0, rows // 16, unroll=8)
     def _(t):
         one = pl.ds(t, 1)
 
@@ -331,9 +331,6 @@
     z = jnp.dot(w_t[...], agg_all[...], preferred_element_type=F32)
     s = 1.0 / (1.0 + jnp.exp(-z))
     grad_z = (cot_all[...].astype(F32) * s * (1.0 + z * (1.0 - s))).astype(BF)
-    grad_agg = jnp.dot(weight[...], grad_z, preferred_element_type=F32)
-    sg_own[...] = (root[:, nodes_of(g)] * grad_agg).astype(BF)
-    send_all(SGS)
     product = lax.dot_general(agg_all[...], grad_z, NT, preferred_element_type=F32)
     chunk = feat // (rings // 2)
     for q in range(xs * rings):
@@ -343,6 +340,9 @@
                 top : top + chunk, (q % 2) * 128 : (q % 2) * 128 + 128
             ].astype(BF)
     send_all(RSUM)
+    grad_agg = jnp.dot(weight[...], grad_z, preferred_element_type=F32)
+    sg_own[...] = (root[:, nodes_of(g)] * grad_agg).astype(BF)
+    send_all(SGS)
     t_in[x * rings + ring] = t_own[x * rings + ring]
     hid_own[...] = (z * s).astype(BF)
     sg[:, nodes_of(g)] = sg_own[rows_of(g), :]
@@ -400,15 +400,11 @@
 
 
 def settle(*refs):
-    kept, sems = refs[6:9], refs[9]
-    arrive = [pltpu.make_async_copy(refs[i], kept[i], sems.at[0, i]) for i in range(3)]
-    leave = [pltpu.make_async_copy(kept[i], refs[3 + i], sems.at[1, i]) for i in range(3)]
-    for copy in arrive:
+    sems = refs[6]
+    copies = [pltpu.make_async_copy(refs[i], refs[3 + i], sems.at[i]) for i in range(3)]
+    for copy in copies:
         copy.start()
-    for i in (2, 0, 1):
-        arrive[i].wait()
-        leave[i].start()
-    for copy in leave:
+    for copy in copies:
         copy.wait()
 
 
@@ -427,9 +423,9 @@
     outs = pl.pallas_call(
             functools.partial(kernel, (blocks, groups, rings)),
             out_shape=(
-                jax.ShapeDtypeStruct((feat, rows), BF),
-                jax.ShapeDtypeStruct((feat, rows), F32),
-                jax.ShapeDtypeStruct((feat, width), F32),
+                vmem((feat, rows), BF),
+                vmem((feat, rows), F32),
+                vmem((feat, width), F32),
             ),
             in_specs=[
                 pl.BlockSpec(memory_space=pl.ANY if i in (0, 1, 4) else vmem) for i in range(5)
@@ -480,11 +476,10 @@
         pl.pallas_call(
             settle,
             out_shape=[jax.ShapeDtypeStruct(o.shape, o.dtype) for o in outs],
-            in_specs=[pl.BlockSpec(memory_space=pl.ANY)] * 3,
+            in_specs=[pl.BlockSpec(memory_space=vmem)] * 3,
             out_specs=[pl.BlockSpec(memory_space=pl.ANY)] * 3,
-            scratch_shapes=[pltpu.VMEM(o.shape, o.dtype) for o in outs]
-            + [pltpu.SemaphoreType.DMA((2, 3))],
-            compiler_params=pltpu.CompilerParams(vmem_limit_bytes=60 * 1024 * 1024),
+            scratch_shapes=[pltpu.SemaphoreType.DMA((3,))],
+            compiler_params=pltpu.CompilerParams(vmem_limit_bytes=1024 * 1024),
         )(*outs)
     )
 

time: 78.4 us -> 79.3 us (1.011)
  Pallas kernels: 77.5 us -> 78.4 us
    pallas_call x1, Pallas kernels: 75.7 us -> 77.6 us  [body(): pl.pallas_call(functools.partial(kernel, (blocks, groups, rings)), out_sh...]
    pallas_call x1, Pallas kernels: 1.78 us -> 0.78 us  [body(): pl.pallas_call(settle, out_shape=[jax.ShapeDtypeStruct(o.shape, o.dtype)...]
where the time goes in v5:
time: 79.3 us; the launch traced here: 79.1 us
  Pallas kernels  78.4 us (99%)
    pallas_call x1, Pallas kernels, body(): pl.pallas_call(functools.partial(kernel, (blocks, groups, rings)), out_sh...  77.6 us

profile of v5, /device:TPU:1, one launch (start us, length us, event | category | flops | bytes accessed | tf_op | source)
XLA Modules:
  0.0 79.1 jit_solution(3263655188885260524)
XLA Ops:
  0.6 77.6 %shard_map.76 = (bf16[32,2048]{1,0:T(8,128)(2,1)S(1)}, f32[32,2048]{1,0:T(8,128)S(1)}, f32[32,256]{1,0:T(8,128)S(1)}) custom-call(bf16[32,2048]{1,0:T(8,128)(2,1)} %feats_in.1, bf16[256,256]{1,0:T(8,128)(2,1)} %weight_in.1, s32[2,2048]{1,0:T(2,128)} %nbr.1, bf16[2,2048]{1,0:T(2,128)(2,1)} %mult.1, bf16[32,2048]{1,0:T(8,128)(2,1)} %cotan_in.1), custom_call_target="tpu_custom_call" | custom-call | tf_op jit(solution)/shard_map/pallas_call | solution.py:423
  78.3 0.8 shard_map.77

commit v6 on v5

--- a/solution.py
+++ b/solution.py
@@ -281,7 +281,7 @@
     zero = jnp.zeros((16, edges), BF)
     ones = jnp.ones((16, edges), BF)
 
-    @pl.loop(0, rows // 16, unroll=8)
+    @pl.loop(0, rows // 16, unroll=16)
     def _(t):
         one = pl.ds(t, 1)
 
@@ -331,6 +331,9 @@
     z = jnp.dot(w_t[...], agg_all[...], preferred_element_type=F32)
     s = 1.0 / (1.0 + jnp.exp(-z))
     grad_z = (cot_all[...].astype(F32) * s * (1.0 + z * (1.0 - s))).astype(BF)
+    grad_agg = jnp.dot(weight[...], grad_z, preferred_element_type=F32)
+    sg_own[...] = (root[:, nodes_of(g)] * grad_agg).astype(BF)
+    send_all(SGS)
     product = lax.dot_general(agg_all[...], grad_z, NT, preferred_element_type=F32)
     chunk = feat // (rings // 2)
     for q in range(xs * rings):
@@ -340,9 +343,6 @@
                 top : top + chunk, (q % 2) * 128 : (q % 2) * 128 + 128
             ].astype(BF)
     send_all(RSUM)
-    grad_agg = jnp.dot(weight[...], grad_z, preferred_element_type=F32)
-    sg_own[...] = (root[:, nodes_of(g)] * grad_agg).astype(BF)
-    send_all(SGS)
     t_in[x * rings + ring] = t_own[x * rings + ring]
     hid_own[...] = (z * s).astype(BF)
     sg[:, nodes_of(g)] = sg_own[rows_of(g), :]
@@ -363,7 +363,7 @@
 
         if off > 0:
             back_copy(off).start()
-        if off == 3:
+        if off == 2:
             wait_all(RSUM)
             total = t_in[0].astype(F32)
             for q in range(1, xs * rings):

time: 79.3 us -> 78.6 us (level)
  no operation moved by 1% of the time
where the time goes in v6:
time: 78.6 us; the launch traced here: 78.4 us
  Pallas kernels  77.7 us (99%)
    pallas_call x1, Pallas kernels, body(): pl.pallas_call(functools.partial(kernel, (blocks, groups, rings)), out_sh...  76.9 us

profile of v6, /device:TPU:1, one launch (start us, length us, event | category | flops | bytes accessed | tf_op | source)
XLA Modules:
  0.0 78.4 jit_solution(11848601721632964197)
XLA Ops:
  0.6 76.9 %shard_map.76 = (bf16[32,2048]{1,0:T(8,128)(2,1)S(1)}, f32[32,2048]{1,0:T(8,128)S(1)}, f32[32,256]{1,0:T(8,128)S(1)}) custom-call(bf16[32,2048]{1,0:T(8,128)(2,1)} %feats_in.1, bf16[256,256]{1,0:T(8,128)(2,1)} %weight_in.1, s32[2,2048]{1,0:T(2,128)} %nbr.1, bf16[2,2048]{1,0:T(2,128)(2,1)} %mult.1, bf16[32,2048]{1,0:T(8,128)(2,1)} %cotan_in.1), custom_call_target="tpu_custom_call" | custom-call | tf_op jit(solution)/shard_map/pallas_call | solution.py:423
  77.6 0.8 shard_map.77

commit v7 on v3

--- a/solution.py
+++ b/solution.py
@@ -405,15 +405,11 @@
 
 
 def settle(*refs):
-    kept, sems = refs[6:9], refs[9]
-    arrive = [pltpu.make_async_copy(refs[i], kept[i], sems.at[0, i]) for i in range(3)]
-    leave = [pltpu.make_async_copy(kept[i], refs[3 + i], sems.at[1, i]) for i in range(3)]
-    for copy in arrive:
+    sems = refs[6]
+    copies = [pltpu.make_async_copy(refs[i], refs[3 + i], sems.at[i]) for i in range(3)]
+    for copy in copies:
         copy.start()
-    for i in (2, 0, 1):
-        arrive[i].wait()
-        leave[i].start()
-    for copy in leave:
+    for copy in copies:
         copy.wait()
 
 
@@ -432,9 +428,9 @@
     outs = pl.pallas_call(
             functools.partial(kernel, (blocks, groups, rings)),
             out_shape=(
-                jax.ShapeDtypeStruct((feat, rows), BF),
-                jax.ShapeDtypeStruct((feat, rows), F32),
-                jax.ShapeDtypeStruct((feat, width), F32),
+                vmem((feat, rows), BF),
+                vmem((feat, rows), F32),
+                vmem((feat, width), F32),
             ),
             in_specs=[
                 pl.BlockSpec(memory_space=pl.ANY if i in (0, 1, 4) else vmem) for i in range(5)
@@ -487,11 +483,10 @@
         pl.pallas_call(
             settle,
             out_shape=[jax.ShapeDtypeStruct(o.shape, o.dtype) for o in outs],
-            in_specs=[pl.BlockSpec(memory_space=pl.ANY)] * 3,
+            in_specs=[pl.BlockSpec(memory_space=vmem)] * 3,
             out_specs=[pl.BlockSpec(memory_space=pl.ANY)] * 3,
-            scratch_shapes=[pltpu.VMEM(o.shape, o.dtype) for o in outs]
-            + [pltpu.SemaphoreType.DMA((2, 3))],
-            compiler_params=pltpu.CompilerParams(vmem_limit_bytes=60 * 1024 * 1024),
+            scratch_shapes=[pltpu.SemaphoreType.DMA((3,))],
+            compiler_params=pltpu.CompilerParams(vmem_limit_bytes=1024 * 1024),
         )(*outs)
     )
 

time: 78.7 us -> 76.9 us (0.977)
  Pallas kernels: 77.8 us -> 76 us
    pallas_call x1, Pallas kernels: 1.78 us -> 0.78 us  [body(): pl.pallas_call(settle, out_shape=[jax.ShapeDtypeStruct(o.shape, o.dtype)...]
where the time goes in v7:
time: 76.9 us; the launch traced here: 76.7 us
  Pallas kernels  76 us (99%)
    pallas_call x1, Pallas kernels, body(): pl.pallas_call(functools.partial(kernel, (blocks, groups, rings)), out_sh...  75.3 us

profile of v7, /device:TPU:1, one launch (start us, length us, event | category | flops | bytes accessed | tf_op | source)
XLA Modules:
  0.0 76.7 jit_solution(2239005753978149320)
XLA Ops:
  0.6 75.3 %shard_map.76 = (bf16[32,2048]{1,0:T(8,128)(2,1)S(1)}, f32[32,2048]{1,0:T(8,128)S(1)}, f32[32,256]{1,0:T(8,128)S(1)}) custom-call(bf16[32,2048]{1,0:T(8,128)(2,1)} %feats_in.1, bf16[256,256]{1,0:T(8,128)(2,1)} %weight_in.1, s32[2,2048]{1,0:T(2,128)} %nbr.1, bf16[2,2048]{1,0:T(2,128)(2,1)} %mult.1, bf16[32,2048]{1,0:T(8,128)(2,1)} %cotan_in.1), custom_call_target="tpu_custom_call" | custom-call | tf_op jit(solution)/shard_map/pallas_call | solution.py:428
  75.9 0.8 %shard_map.77 = (bf16[32,2048]{1,0:T(8,128)(2,1)}, f32[32,2048]{1,0:T(8,128)}, f32[32,256]{1,0:T(8,128)}) custom-call(bf16[32,2048]{1,0:T(8,128)(2,1)S(1)} %get-tuple-element.6.refs_0_, f32[32,2048]{1,0:T(8,128)S(1)} %get-tuple-element.7.refs_1_, f32[32,256]{1,0:T(8,128)S(1)} %get-tuple-element.8.refs_2_), custom_call_target="tpu_custom_call" | custom-call | tf_op jit(solution)/shard_map/pallas_call | solution.py:483
